TPU v7x, 128 devices: a whole 4x4x4 slice. The times are simulated.
128 devices in a mesh: member: 8 (over y, z_lo), space: 16 (over z_hi, x, core).
Axes of the slice: x: 4, y: 4, z: 4 (z_hi: 2, z_lo: 2; z = z_hi * 2 + z_lo), core: 2. Of those that a mesh axis runs over, the one named last changes fastest.
Arguments:
- tokens: bfloat16 [16, 2048, 1024], P('member', 'space'), may hold values from -6 to 6
- w_qkv: bfloat16 [1024, 3072], replicated, may hold values from -0.1875 to 0.1875
- w_out: bfloat16 [1024, 1024], replicated, may hold values from -1.5 to 1.5
- w_hidden: bfloat16 [1024, 1024], replicated, may hold values from -0.1875 to 0.1875
- decoder_readout_matrix: bfloat16 [1024, 128], replicated, may hold values from -0.1875 to 0.1875
- edge_token: int32 [16384, 3], P('space'), may hold values from 0 to 2047, as said below
- edge_weight: float32 [16384, 3], P('space'), may hold values from 0.2 to 1
- truth_state: float32 [16384, 128], P('space'), may hold values from -6 to 6
- area: float32 [16384], P('space'), may hold values from 0.3 to 3
Outputs:
- grad_tokens: bfloat16 [16, 2048, 1024], P('member', 'space')
- grad_qkv_w: float32 [1024, 3072], P(('member', 'space'))
- grad_out_w: float32 [1024, 1024], P(('member', 'space'))
- grad_hidden_w: float32 [1024, 1024], P(('member', 'space'))
- decoder_readout_derivative: float32 [1024, 128], P(('member', 'space'))
Inputs may be any that keep to these rules, and one draw needn't show every extreme that they name: edge_token[c, e] // 128 == c // 1024: a cell's edges reach tokens of its own block.
All inputs are finite; a program needn't handle non-finite values.
Results may differ from a plain program's by a relative error of at most 0.017.
Values may be sent and summed in bfloat16 or wider, within the bound.
A program may use at most 192 MiB of HBM per device.

v0:
```python
import functools
import math
import types

import jax
import jax.numpy as jnp
from jax import lax
from jax.experimental import pallas as pl
from jax.experimental.pallas import tpu as pltpu
from jax.sharding import PartitionSpec as P

EPS = 1e-05
ALPHA = 0.95
DELTA = 0.1


MESH = pl.DeviceIdType.MESH


class Place:
    def __init__(self):
        member, space = lax.axis_index("member"), lax.axis_index("space")
        self.member, self.space = member, space
        self.y, z_lo = member // 2, member % 2
        z_hi = space // 8
        self.x, self.core = (space // 2) % 4, space % 2
        self.z = z_hi * 2 + z_lo
        self.partner = (member, space + 1 - 2 * self.core)

    def ring(self, axis):
        return {"x": self.x, "y": self.y, "z": self.z}[axis]

    def device(self, axis, j):
        if axis == "x":
            return (self.member, (self.space // 8) * 8 + j * 2 + self.core)
        if axis == "y":
            return (j * 2 + self.member % 2, self.space)
        return ((self.member // 2) * 2 + j % 2, (j // 2) * 8 + self.space % 8)

    def neighbours(self):
        found = []
        for axis in "xyz":
            i = self.ring(axis)
            found += [self.device(axis, (i + 1) % 4), self.device(axis, (i + 3) % 4)]
        return found


def entry_barrier(devices):
    barrier = pltpu.get_barrier_semaphore()
    for device in devices:
        pl.semaphore_signal(barrier, inc=1, device_id=device, device_id_type=MESH)
    pl.semaphore_wait(barrier, len(devices))


ORDERS = (
    (
        ("x", (4, 2, 2), lambda j, r: (*r, j)),
        ("y", (2, 2), lambda j, r: (j, *r)),
        ("z", (), lambda j, r: (j % 2, j // 2)),
    ),
    (
        ("y", (2, 2, 4), lambda j, r: (j, *r)),
        ("z", (4,), lambda j, r: (j % 2, j // 2, *r)),
        ("x", (), lambda j, r: (j,)),
    ),
    (
        ("z", (4, 4), lambda j, r: (r[0], j % 2, j // 2, r[1])),
        ("x", (4,), lambda j, r: (r[0], j)),
        ("y", (), lambda j, r: (j,)),
    ),
)
FULL = (4, 2, 2, 4)


def first_columns(width):
    return width // 128 // 2 * 128


def sum_scratch(width):
    low = first_columns(width)
    shapes = []
    for order in ORDERS:
        for phase, (_, rest, _) in enumerate(order):
            for columns in (width, width, low, width - low):
                shapes.append(pltpu.VMEM((*rest, 16, columns), jnp.bfloat16))
            if phase < 2:
                shapes.append(pltpu.VMEM((*rest, 16, width), jnp.bfloat16))
    return shapes + [pltpu.SemaphoreType.DMA((54,)), pltpu.SemaphoreType.DMA((54,))]


def over(dims, body):
    if len(dims) <= 1:
        body((slice(None),) * len(dims))
        return
    count = math.prod(dims[:-1])

    def step(n, carry):
        index = []
        for size in reversed(dims[:-1]):
            index.insert(0, lax.rem(n, size))
            n = n // size
        body((*index, slice(None)))
        return carry

    lax.fori_loop(0, count, step, 0)


class RingSum:
    def __init__(self, place, width, parts, scratch, finish):
        self.place, self.width, self.low = place, width, first_columns(width)
        scratch = list(scratch)
        self.recv, self.send = scratch.pop(), scratch.pop()
        self.slots = []
        for _ in range(3):
            self.slots.append([])
            for phase in range(3):
                count = 5 if phase < 2 else 4
                self.slots[-1].append(scratch[:count])
                scratch = scratch[count:]
        self.data = [[part] for part in parts]
        for part in range(3):
            self.data[part] += [self.slots[part][phase][4] for phase in range(2)]
        self.finish = finish
        self.copies = {}

    def copy(self, part, phase, message, source, target, device):
        sem = (part * 3 + phase) * 6 + message
        made = pltpu.make_async_remote_copy(
            src_ref=source, dst_ref=target, send_sem=self.send.at[sem], recv_sem=self.recv.at[sem],
            device_id=device, device_id_type=MESH,
        )
        made.start()
        self.copies[part, phase, message] = made

    def view(self, part, phase, j, low):
        _, rest, at = ORDERS[part][phase]
        columns = pl.ds(0, self.low) if low else pl.ds(self.low, self.width - self.low)
        return self.data[part][phase].at[(*at(j, (slice(None),) * len(rest)), slice(None), columns)]

    def around(self, part, phase):
        axis = ORDERS[part][phase][0]
        i = self.place.ring(axis)
        right, left = (i + 1) % 4, (i + 3) % 4
        return i, right, left, (i + 2) % 4, self.place.device(axis, right), self.place.device(axis, left)

    def open(self, part, phase):
        _, right, left, opposite, to_right, to_left = self.around(part, phase)
        from_left, from_right, relay_left, relay_right = self.slots[part][phase][:4]
        low, high = pl.ds(0, self.low), pl.ds(self.low, self.width - self.low)
        self.copy(part, phase, 0, self.view(part, phase, opposite, True), relay_left, to_right)
        self.copy(part, phase, 1, self.view(part, phase, opposite, False), relay_right, to_left)
        self.copy(part, phase, 2, self.view(part, phase, right, False), from_left.at[..., high], to_right)
        self.copy(part, phase, 3, self.view(part, phase, left, True), from_right.at[..., low], to_left)

    def relay(self, part, phase):
        _, right, left, _, to_right, to_left = self.around(part, phase)
        _, rest, at = ORDERS[part][phase]
        from_left, from_right, relay_left, relay_right = self.slots[part][phase][:4]
        low, high = pl.ds(0, self.low), pl.ds(self.low, self.width - self.low)
        data = self.data[part][phase]
        for message, j, columns, relayed in ((0, right, low, relay_left), (1, left, high, relay_right)):
            self.copies[part, phase, message].wait_recv()

            def add(r, j=j, columns=columns, relayed=relayed):
                here = (*at(j, r), slice(None), columns)
                there = (*r, slice(None), slice(None))
                both = data[here].astype(jnp.float32) + relayed[there].astype(jnp.float32)
                data[here] = both.astype(jnp.bfloat16)

            over(rest, add)
            if message == 0:
                self.copy(part, phase, 4, self.view(part, phase, right, True), from_left.at[..., low], to_right)
            else:
                self.copy(part, phase, 5, self.view(part, phase, left, False), from_right.at[..., high], to_left)

    def close(self, part, phase):
        i = self.around(part, phase)[0]
        _, rest, at = ORDERS[part][phase]
        from_left, from_right = self.slots[part][phase][:2]
        data = self.data[part][phase]
        for message in (2, 3, 4, 5):
            self.copies[part, phase, message].wait_recv()

        def add(r):
            there = (*r, slice(None), slice(None))
            total = data[(*at(i, r), slice(None), slice(None))].astype(jnp.float32)
            total = total + from_left[there].astype(jnp.float32) + from_right[there].astype(jnp.float32)
            if phase < 2:
                self.data[part][phase + 1][there] = total.astype(jnp.bfloat16)
            else:
                self.finish(part, total)

        over(rest, add)

    def steps(self):
        for phase in range(3):
            for part in range(3):
                self.relay(part, phase)
                yield
            for part in range(3):
                self.close(part, phase)
                if phase < 2:
                    self.open(part, phase + 1)
                yield

    def drain(self):
        for made in self.copies.values():
            made.wait_send()


NT = (((1,), (1,)), ((), ()))
TN = (((0,), (0,)), ((), ()))


def dot_nn(a, b):
    return jnp.dot(a, b, preferred_element_type=jnp.float32)


def dot_nt(a, b):
    return lax.dot_general(a, b, NT, preferred_element_type=jnp.float32)


def dot_tn(a, b):
    return lax.dot_general(a, b, TN, preferred_element_type=jnp.float32)


def gelu_both(x):
    bell = jnp.exp(-0.5 * (x * x))
    t = 1.0 / (1.0 + (0.3275911 / math.sqrt(2.0)) * jnp.abs(x))
    poly = t * (
        0.5 * 0.254829592
        + t * (-0.5 * 0.284496736 + t * (0.5 * 1.421413741 + t * (-0.5 * 1.453152027 + t * (0.5 * 1.061405429))))
    )
    tail = poly * bell
    share = jnp.where(x >= 0.0, 1.0 - tail, tail)
    return x * share, share + x * (bell * (1.0 / math.sqrt(2.0 * math.pi)))


def norm_back(objective_derivative, normal_hat, inverse):
    first = jnp.mean(objective_derivative, axis=-1, keepdims=True)
    second = jnp.mean(objective_derivative * normal_hat, axis=-1, keepdims=True)
    return inverse * (objective_derivative - first - normal_hat * second)


def normalised(values):
    wide = values.astype(jnp.float32)
    centre = wide - jnp.mean(wide, axis=-1, keepdims=True)
    inverse = lax.rsqrt(jnp.mean(centre * centre, axis=-1, keepdims=True) + EPS)
    return centre * inverse, inverse


def in_columns(count=4):
    return [slice(part * 256, part * 256 + 256) for part in range(count)]


def kernel(names, *refs):
    r = types.SimpleNamespace(**dict(zip(names, refs)))
    ring_scratch = refs[len(names) :]
    place = Place()
    member, space, core = place.member, place.space, place.core

    loads = [
        pltpu.make_async_copy(
            r.w_qkv_hbm.at[:, pl.ds(part * 1024, 1024)], r.w_qkv.at[:, pl.ds(part * 1024, 1024)], r.load_sems.at[part]
        )
        for part in range(3)
    ]
    loads.append(pltpu.make_async_copy(r.w_out_hbm, r.w_out, r.load_sems.at[3]))
    loads.append(pltpu.make_async_copy(r.w_hidden_hbm, r.w_hidden, r.load_sems.at[4]))
    loads.append(pltpu.make_async_copy(
        r.truth_hbm.at[pl.ds(pl.multiple_of(member * 128, 128), 128), :], r.truth, r.load_sems.at[5]
    ))
    for load in loads:
        load.start()

    above, below = (member, lax.rem(space + 1, 16)), (member, lax.rem(space + 15, 16))
    others = [lax.rem(member + k, 8) for k in range(1, 8)]
    entry_barrier([above, below, place.partner, *place.neighbours(), *[(other, space) for other in others]])
    sent_copies = []

    def push(source, target, sems, i, device):
        made = pltpu.make_async_remote_copy(
            src_ref=source, dst_ref=target, send_sem=sems.at[(0, *i)], recv_sem=sems.at[(1, *i)],
            device_id=device, device_id_type=MESH,
        )
        made.start()
        sent_copies.append(made)
        return made

    halo_tokens = []
    for m in range(2):
        halo_tokens.append(push(
            r.tokens.at[pl.ds(m * 128 + 64, 64)], r.halo.at[m, pl.ds(0, 64)], r.token_sems, (0, m), above
        ))
        halo_tokens.append(push(
            r.tokens.at[pl.ds(m * 128, 64)], r.halo.at[m, pl.ds(64, 64)], r.token_sems, (1, m), below
        ))

    pair_count = [0]

    def pair(source, target):
        pair_count[0] += 1
        return push(source, target, r.pair_sems, (pair_count[0] - 1,), place.partner)

    for block in range(4):
        rows = slice(block * 64, block * 64 + 64)
        r.normed[rows, :] = normalised(r.tokens[rows, :])[0].astype(jnp.bfloat16)
    normed_here = pair(r.normed, r.normed_2)
    loads[0].wait()
    for columns in in_columns():
        r.queries[:, columns] = dot_nn(r.normed[...], r.w_qkv[:, columns]).astype(jnp.bfloat16)

    row = lax.broadcasted_iota(jnp.int32, (256, 256), 0) % 128
    key = lax.broadcasted_iota(jnp.int32, (256, 256), 1)
    token = space * 128 - 64 + key
    inside = (key >= row) & (key <= row + 128) & (token >= 0) & (token < 2048)
    r.window[...] = jnp.where(inside, 1.0, 0.0)
    for group, columns in enumerate(in_columns()):
        local = r.edge_token[:, columns] - space * 128
        weight = r.edge_weight[:, columns]
        places = lax.broadcasted_iota(jnp.int32, (128, 256), 0)
        matrix = jnp.zeros((128, 256), jnp.float32)
        for slot in range(3):
            matrix = matrix + jnp.where(local[slot : slot + 1] == places, weight[slot : slot + 1], 0.0)
        high = matrix.astype(jnp.bfloat16)
        both = jnp.concatenate([high, (matrix - high.astype(jnp.float32)).astype(jnp.bfloat16)], axis=0)
        r.edges_t[group] = both
        r.edges[group] = both.T

    for made in halo_tokens:
        made.wait_recv()
    for m in range(2):
        r.halo[m] = normalised(r.halo[m])[0].astype(jnp.bfloat16)
    every = jnp.concatenate([r.normed[...], r.halo[0], r.halo[1]], axis=0)
    for part in range(2):
        loads[1 + part].wait()
        for n in range(4):
            at = slice(part * 1024 + n * 256, part * 1024 + n * 256 + 256)
            value = dot_nn(every, r.w_qkv[:, slice(at.start + 1024, at.stop + 1024)]).astype(jnp.bfloat16)
            for m in range(2):
                edge = 256 + m * 128
                r.kv[m, 0:64, at] = value[edge : edge + 64]
                r.kv[m, 64:192, at] = value[m * 128 : m * 128 + 128]
                r.kv[m, 192:256, at] = value[edge + 64 : edge + 128]

    first = lax.broadcasted_iota(jnp.int32, (128, 128), 1) < 64

    def stacked(value):
        zero = jnp.zeros_like(value)
        return jnp.concatenate([jnp.where(first, value, zero), jnp.where(first, zero, value)], axis=0)

    def attend(i, carry):
        m, n = i // 8, lax.rem(i, 8)
        start = pl.multiple_of(n * 128, 128)
        columns, values = pl.ds(start, 128), pl.ds(start + 1024, 128)
        token_rows = pl.ds(pl.multiple_of(m * 128, 128), 128)
        scores = dot_nt(stacked(r.queries[token_rows, columns]), r.kv[m, :, columns])
        expo = jnp.where(r.window[...] > 0.0, jnp.exp(scores * 0.125), 0.0)
        probs = expo / jnp.sum(expo, axis=-1, keepdims=True)
        r.probs[i] = probs
        result = dot_nn(probs.astype(jnp.bfloat16), r.kv[m, :, values])
        r.att[token_rows, columns] = jnp.where(first, result[:128], result[128:]).astype(jnp.bfloat16)
        return carry

    lax.fori_loop(0, 16, attend, 0, unroll=2)
    att_here = pair(r.att, r.att_2)
    loads[3].wait()
    for columns in in_columns():
        value = r.tokens[:, columns].astype(jnp.float32) + dot_nn(r.att[...], r.w_out[:, columns])
        r.states[:, columns] = value.astype(jnp.bfloat16)
    states_here = pair(r.states, r.states_2)
    loads[4].wait()
    for columns in in_columns():
        value = dot_nn(r.states[...], r.w_hidden[:, columns]).astype(jnp.bfloat16)
        for m in range(2):
            r.hidden[m, 0:128, columns] = value[m * 128 : m * 128 + 128]
            r.hidden[m, 128:256, columns] = value[m * 128 : m * 128 + 128]

    home = member // 2

    def give(source, target, i, to):
        return pltpu.make_async_remote_copy(
            src_ref=source.at[to], dst_ref=target.at[member], send_sem=r.member_sems.at[i, 0, to],
            recv_sem=r.member_sems.at[i, 1, member], device_id=(to, space), device_id_type=MESH,
        )

    def take(target, i, source):
        return pltpu.make_async_remote_copy(
            src_ref=target.at[source], dst_ref=target.at[source], send_sem=r.member_sems.at[i, 0, source],
            recv_sem=r.member_sems.at[i, 1, source], device_id=(source, space), device_id_type=MESH,
        )

    for n in range(4):
        group = lax.rem(home + 1 + n, 4)

        def forward(b, carry, group=group):
            forecast = jnp.zeros((256, 128), jnp.float32)
            for columns in in_columns():
                value, derivative = gelu_both(dot_nn(r.edges[group], r.hidden[b, :, columns]))
                value = value.astype(jnp.bfloat16)
                r.active[b, group, :, columns] = value
                r.slope[b, group, :, columns] = derivative.astype(jnp.bfloat16)
                forecast = forecast + dot_nn(value, r.readout[columns, :])
            r.sent[2 * group, b] = forecast[:128].astype(jnp.bfloat16)
            r.sent[2 * group + 1, b] = forecast[128:].astype(jnp.bfloat16)
            return carry

        lax.fori_loop(0, 2, forward, 0)
        if n < 3:
            give(r.sent, r.held, 0, 2 * group).start()
            give(r.sent, r.held, 0, 2 * group + 1).start()
        else:
            give(r.sent, r.held, 0, 2 * group + 1 - lax.rem(member, 2)).start()
            r.held[member] = r.sent[member]
    r.area_here[...] = jnp.broadcast_to(r.area[pl.ds(member, 1), :], (128, 128)).T
    loads[5].wait()
    for other in others:
        take(r.held, 0, other).wait_recv()

    multiplier = math.sqrt(16 / 16384)
    eps_fair = (1.0 - ALPHA) / 16

    def score(block, carry):
        rows = pl.ds(pl.multiple_of(block * 16, 16), 16)
        whole = [r.held[m // 2, m % 2, rows, :].astype(jnp.float32) for m in range(16)]
        truth, area = r.truth[rows, :], r.area_here[rows, :]
        found = [[] for _ in range(16)]
        for half in (slice(0, 8), slice(8, 16)):
            values = [value[half] for value in whole]
            spread = [None] * 16
            for j in range(16):
                for k in range(j + 1, 16):
                    d = values[j] - values[k]
                    s = d * lax.rsqrt(d * d + DELTA * DELTA)
                    spread[j] = s if spread[j] is None else spread[j] + s
                    spread[k] = -s if spread[k] is None else spread[k] - s
            for j in range(16):
                d = values[j] - truth[half]
                s = d * lax.rsqrt(d * d + DELTA * DELTA)
                found[j].append(
                    multiplier * area[half] * (s / 16 - (1.0 - eps_fair) / (16 * 15) * spread[j])
                )
        for j in range(16):
            r.sent_back[j // 2, j % 2, rows, :] = jnp.concatenate(found[j], axis=0).astype(jnp.bfloat16)
        return carry

    lax.fori_loop(0, 8, score, 0)
    for other in others:
        give(r.sent_back, r.held_back, 1, other).start()
    r.held_back[member] = r.sent_back[member]

    r.gathered[...] = jnp.zeros_like(r.gathered)
    r.turned[...] = jnp.zeros_like(r.turned)
    for n in range(4):
        group = lax.rem(home + n, 4)
        if n == 0:
            take(r.held_back, 1, 2 * group + 1 - lax.rem(member, 2)).wait_recv()
        else:
            take(r.held_back, 1, 2 * group).wait_recv()
            take(r.held_back, 1, 2 * group + 1).wait_recv()

        def backward(b, carry, group=group):
            grad = jnp.concatenate([r.held_back[2 * group, b], r.held_back[2 * group + 1, b]], axis=0)
            token_rows = pl.ds(pl.multiple_of(b * 128, 128), 128)
            for columns in in_columns():
                hidden = dot_nt(grad, r.readout[columns, :])
                grad_pre = (hidden * r.slope[b, group, :, columns].astype(jnp.float32)).astype(jnp.bfloat16)
                both = dot_nn(r.edges_t[group], grad_pre)
                r.gathered[token_rows, columns] += both[:128] + both[128:]
                r.turned[:, columns] += dot_tn(grad, r.active[b, group, :, columns])
            return carry

        lax.fori_loop(0, 2, backward, 0)

    mine = pl.ds(pl.multiple_of(core * 512, 512), 512)
    other_half = pl.ds(pl.multiple_of((1 - core) * 512, 512), 512)
    high = r.gathered[...].astype(jnp.bfloat16)
    r.gather_b[...] = high
    gather_here = pair(r.gather_b.at[:, other_half], r.gather_2)
    r.readout_grad[...] = r.turned[...].T.astype(jnp.bfloat16)
    readout_here = pair(r.readout_grad, r.readout_2)
    low = (r.gathered[...] - high.astype(jnp.float32)).astype(jnp.bfloat16)
    for rows in in_columns():
        weights = r.w_hidden[rows, :]
        value = dot_nt(high, weights) + dot_nt(low, weights)
        r.grad_s[:, rows] = value
        r.grad_sb[:, rows] = value.astype(jnp.bfloat16)
    grad_s_here = pair(r.grad_sb.at[:, other_half], r.grad_s2)

    def early_tile(tile, y, value):
        columns = slice(tile % 3 * 128, tile % 3 * 128 + 128)
        r.early_data[tile // 3, y, :, :, :, :, columns] = value.astype(jnp.bfloat16).reshape(2, 2, 4, 16, 128)

    states_here.wait_recv()
    gather_here.wait_recv()
    for y, rows in enumerate(in_columns()):
        value = dot_tn(r.states[:, rows], r.gather_b[:, mine]) + dot_tn(r.states_2[:, rows], r.gather_2[...])
        for tile in range(4):
            early_tile(tile, y, value[:, tile * 128 : tile * 128 + 128])
    readout_here.wait_recv()
    for y, rows in enumerate(in_columns()):
        early_tile(8, y, r.readout_grad[rows, :].astype(jnp.float32) + r.readout_2[rows, :].astype(jnp.float32))
    att_here.wait_recv()
    grad_s_here.wait_recv()
    for y, rows in enumerate(in_columns()):
        value = dot_tn(r.att[:, rows], r.grad_sb[:, mine]) + dot_tn(r.att_2[:, rows], r.grad_s2[...])
        for tile in range(4):
            early_tile(4 + tile, y, value[:, tile * 128 : tile * 128 + 128])

    def early_finish(part, total):
        r.early_final[:, :, part * 384 : part * 384 + 384] = total.reshape(2, 8, 384)

    def late_finish(part, total):
        r.late_final[:, :, part * 512 : part * 512 + 512] = total.reshape(2, 8, 512)

    split = len(ring_scratch) // 2
    early = RingSum(place, 384, [r.early_data.at[part] for part in range(3)], ring_scratch[:split], early_finish)
    late = RingSum(place, 512, [r.late_data.at[part] for part in range(3)], ring_scratch[split:], late_finish)
    for part in range(3):
        early.open(part, 0)
    early_steps = early.steps()

    for rows in in_columns():
        r.grad_att[:, rows] = dot_nt(r.grad_sb[...], r.w_out[rows, :]).astype(jnp.bfloat16)

    def attend_back(m, n, carry):
        start = pl.multiple_of(n * 128, 128)
        columns, values = pl.ds(start, 128), pl.ds(start + 1024, 128)
        token_rows = pl.ds(m * 128, 128)
        queries = stacked(r.queries[token_rows, columns])
        grads = stacked(r.grad_att[token_rows, columns])
        probs = r.probs[m * 8 + n]
        dprob = dot_nt(grads, r.kv[m, :, values])
        inner = jnp.sum(probs * dprob, axis=-1, keepdims=True)
        dscore = (probs * (dprob - inner) * 0.125).astype(jnp.bfloat16)
        grad_q = dot_nn(dscore, r.kv[m, :, columns])
        r.grad_qkv[token_rows, columns] = jnp.where(first, grad_q[:128], grad_q[128:]).astype(jnp.bfloat16)
        for value, at in (
            (dot_tn(dscore, queries), columns), (dot_tn(probs.astype(jnp.bfloat16), grads), values)
        ):
            r.lower[m, :, at] = value[:64].astype(jnp.bfloat16)
            r.middle[token_rows, at] = value[64:192]
            r.upper[m, :, at] = value[192:].astype(jnp.bfloat16)
        return carry

    halos = []
    for m in range(2):
        for half in range(2):
            lax.fori_loop(half * 4, half * 4 + 4, functools.partial(attend_back, m), 0, unroll=2)
            for _ in range(4):
                next(early_steps, None)
        halos.append(push(r.lower.at[m], r.from_above.at[m], r.halo_sems, (0, m), below))
        halos.append(push(r.upper.at[m], r.from_below.at[m], r.halo_sems, (1, m), above))

    def swap(part):
        at = pl.ds(pl.multiple_of(part * 1024 + (1 - core) * 512, 512), 512)
        return pair(r.grad_qkv.at[:, at], r.grad_qkv2.at[part])

    def late_product(part):
        own = r.grad_qkv[:, pl.ds(pl.multiple_of(part * 1024 + core * 512, 512), 512)]
        for y, rows in enumerate(in_columns()):
            value = dot_tn(r.normed[:, rows], own) + dot_tn(r.normed_2[:, rows], r.grad_qkv2[part])
            r.late_data[part, y] = value.astype(jnp.bfloat16).reshape(2, 2, 4, 16, 512)
        late.open(part, 0)

    swaps = [swap(0)]
    normed_here.wait_recv()
    swaps[0].wait_recv()
    late_product(0)
    for made in halos:
        made.wait_recv()
    for m in range(2):
        low_rows, high_rows = slice(m * 128, m * 128 + 64), slice(m * 128 + 64, m * 128 + 128)
        for part in range(2):
            at, into = slice(part * 1024, part * 1024 + 1024), slice(part * 1024 + 1024, part * 1024 + 2048)
            for rows, arrived in ((low_rows, r.from_below), (high_rows, r.from_above)):
                total = r.middle[rows, at] + arrived[m, :, at].astype(jnp.float32)
                r.grad_qkv[rows, into] = total.astype(jnp.bfloat16)
    swaps += [swap(1), swap(2)]
    for _ in early_steps:
        pass
    final_sums = [push(r.early_final.at[1 - core], r.early_other, r.final_sems, (0,), place.partner)]
    for part in (1, 2):
        swaps[part].wait_recv()
        late_product(part)
    late_steps = late.steps()
    for rows in in_columns():
        r.middle[:, rows] = dot_nt(r.grad_qkv[...], r.w_qkv[rows, :])
        next(late_steps, None)
        next(late_steps, None)
    for block in range(4):
        rows = slice(block * 64, block * 64 + 64)
        normal_hat, inverse = normalised(r.tokens[rows, :])
        back = norm_back(r.middle[rows, :1024], normal_hat, inverse)
        r.grad_tokens[rows, :] = (r.grad_s[rows, :] + back).astype(jnp.bfloat16)
    for _ in late_steps:
        pass
    final_sums.append(push(r.late_final.at[1 - core], r.late_other, r.final_sems, (1,), place.partner))

    yours = pl.ds(pl.multiple_of((1 - core) * 512, 512), 512)
    r.grad_hidden_w[:, mine] = r.early_final[core, :, :512]
    r.grad_out_w[:, mine] = r.early_final[core, :, 512:1024]
    r.grad_readout[...] = r.early_final[core, :, 1024:]
    final_sums[0].wait_recv()
    r.grad_hidden_w[:, yours] = r.early_other[:, :512]
    r.grad_out_w[:, yours] = r.early_other[:, 512:1024]
    final_sums[1].wait_recv()
    for part in range(3):
        at = slice(part * 512, part * 512 + 512)
        for half, rows in ((core, r.late_final[core, :, at]), (1 - core, r.late_other[:, at])):
            r.grad_qkv_w[:, pl.ds(pl.multiple_of(part * 1024 + half * 512, 512), 512)] = rows
    for made in sent_copies:
        made.wait_send()
    for other in others:
        give(r.sent, r.held, 0, other).wait_send()
        give(r.sent_back, r.held_back, 1, other).wait_send()
    early.drain()
    late.drain()


def on_device(
    tokens, w_qkv, w_out, w_hidden, decoder_readout_matrix, edge_token, edge_weight, truth_state, area
):
    vmem, anywhere = pl.BlockSpec(memory_space=pltpu.VMEM), pl.BlockSpec(memory_space=pl.ANY)
    dma = pltpu.SemaphoreType.DMA

    def b16(*shape):
        return pltpu.VMEM(shape, jnp.bfloat16)

    def f32(*shape):
        return pltpu.VMEM(shape, jnp.float32)

    inputs = {
        "tokens": (tokens.reshape(256, 1024), vmem),
        "w_qkv_hbm": (w_qkv, anywhere),
        "w_out_hbm": (w_out, anywhere),
        "w_hidden_hbm": (w_hidden, anywhere),
        "readout": (decoder_readout_matrix, vmem),
        "edge_token": (edge_token.T, vmem),
        "edge_weight": (edge_weight.T, vmem),
        "truth_hbm": (truth_state, anywhere),
        "area": (area.reshape(8, 128), vmem),
    }
    outputs = {
        "grad_tokens": jax.ShapeDtypeStruct((256, 1024), jnp.bfloat16),
        "grad_qkv_w": jax.ShapeDtypeStruct((8, 3072), jnp.float32),
        "grad_out_w": jax.ShapeDtypeStruct((8, 1024), jnp.float32),
        "grad_hidden_w": jax.ShapeDtypeStruct((8, 1024), jnp.float32),
        "grad_readout": jax.ShapeDtypeStruct((8, 128), jnp.float32),
    }
    scratch = {
        "w_qkv": b16(1024, 3072), "w_out": b16(1024, 1024), "w_hidden": b16(1024, 1024), "truth": f32(128, 128),
        "area_here": f32(128, 128), "halo": b16(2, 128, 1024), "normed": b16(256, 1024), "normed_2": b16(256, 1024),
        "queries": b16(256, 1024), "kv": b16(2, 256, 2048), "window": f32(256, 256), "probs": f32(16, 256, 256),
        "att": b16(256, 1024), "att_2": b16(256, 1024), "states": b16(256, 1024), "states_2": b16(256, 1024),
        "hidden": b16(2, 256, 1024), "edges": b16(4, 256, 256), "edges_t": b16(4, 256, 256),
        "active": b16(2, 4, 256, 1024), "slope": b16(2, 4, 256, 1024),
        "sent": b16(8, 2, 128, 128), "held": b16(8, 2, 128, 128),
        "sent_back": b16(8, 2, 128, 128), "held_back": b16(8, 2, 128, 128), "turned": f32(128, 1024),
        "gathered": f32(256, 1024), "gather_b": b16(256, 1024), "gather_2": b16(256, 512),
        "grad_s": f32(256, 1024), "grad_sb": b16(256, 1024), "grad_s2": b16(256, 512), "grad_att": b16(256, 1024),
        "readout_grad": b16(1024, 128), "readout_2": b16(1024, 128), "grad_qkv": b16(256, 3072),
        "grad_qkv2": b16(3, 256, 512), "middle": f32(256, 2048), "lower": b16(2, 64, 2048), "upper": b16(2, 64, 2048),
        "from_above": b16(2, 64, 2048), "from_below": b16(2, 64, 2048),
        "early_data": b16(3, *FULL, 16, 384), "late_data": b16(3, *FULL, 16, 512),
        "early_final": f32(2, 8, 1152), "late_final": f32(2, 8, 1536),
        "early_other": f32(8, 1152), "late_other": f32(8, 1536),
        "load_sems": dma((6,)), "token_sems": dma((2, 2, 2)), "pair_sems": dma((2, 9)), "halo_sems": dma((2, 2, 2)),
        "member_sems": dma((2, 2, 8)), "final_sems": dma((2, 2)),
    }
    names = [*inputs, *outputs, *scratch]
    results = pl.pallas_call(
        functools.partial(kernel, names),
        out_shape=tuple(outputs.values()),
        in_specs=[spec for _, spec in inputs.values()],
        out_specs=[vmem] * len(outputs),
        scratch_shapes=[*scratch.values(), *sum_scratch(384), *sum_scratch(512)],
        compiler_params=pltpu.CompilerParams(
            collective_id=0, has_side_effects=True, vmem_limit_bytes=62 * 2**20
        ),
    )(*[value for value, _ in inputs.values()])
    return (results[0].reshape(tokens.shape), *results[1:])


def solution(mesh):
    in_specs = (
        P("member", "space", None),
        P(),
        P(),
        P(),
        P(),
        P("space", None),
        P("space", None),
        P("space", None),
        P("space"),
    )
    out_specs = (
        P("member", "space", None),
        P(("member", "space"), None),
        P(("member", "space"), None),
        P(("member", "space"), None),
        P(("member", "space"), None),
    )
    return jax.shard_map(
        on_device, mesh=mesh, in_specs=in_specs, out_specs=out_specs, check_vma=False
    )
```

profile of v0, /device:TPU:1, one launch (start us, length us, event | category | flops | bytes accessed | tf_op | source)
XLA Modules:
  0.0 134.8 jit_solution(4719757750190765244)
XLA Ops:
  0.6 126.7 %shard_map.128 = (bf16[256,1024]{1,0:T(8,128)(2,1)}, f32[8,3072]{1,0:T(8,128)}, f32[8,1024]{1,0:T(8,128)}, f32[8,1024]{1,0:T(8,128)}, f32[8,128]{1,0:T(8,128)}) custom-call(bf16[256,1024]{1,0:T(8,128)(2,1)} %bitcast.6, bf16[1024,3072]{1,0:T(8,128)(2,1)} %refs_1_.1, bf16[1024,1024]{1,0:T(8,128)(2,1)} %refs_2_.1, bf16[1024,1024]{1,0:T(8,128)(2,1)} %refs_3_.1, ...), custom_call_target="tpu_custom_call" | custom-call | tf_op jit(solution)/shard_map/pallas_call | solution.py:672
  127.4 1.9 %copy.19 = bf16[2,128,1024]{2,1,0:T(8,128)(2,1)} copy(bf16[2,128,1024]{2,1,0:T(8,128)(2,1)} %bitcast.5) | data formatting | bytes 1048576
  129.2 1.5 %copy.20 = f32[8,3072]{1,0:T(8,128)} copy(f32[8,3072]{1,0:T(8,128)} %get-tuple-element.21) | data formatting | bytes 196608
  130.8 1.4 %copy.21 = f32[8,1024]{1,0:T(8,128)} copy(f32[8,1024]{1,0:T(8,128)} %get-tuple-element.22) | data formatting | bytes 65536
  132.2 1.4 %copy.22 = f32[8,1024]{1,0:T(8,128)} copy(f32[8,1024]{1,0:T(8,128)} %get-tuple-element.23) | data formatting | bytes 65536
  133.5 1.3 copy.23
where the time goes:
time: 135 us
  Pallas kernels  127 us (94%)
  local copies, waits for them, and re-layouts  7.43 us (6%)
    pallas_call x1, Pallas kernels, on_device(): pl.pallas_call(functools.partial(kernel, names), out_shape=tuple(outputs....  127 us
    unnamed x5, local copies, waits for them, and re-layouts  7.43 us

commit v1 on v0

--- a/solution.py
+++ b/solution.py
@@ -81,10 +81,9 @@
     shapes = []
     for order in ORDERS:
         for phase, (_, rest, _) in enumerate(order):
-            for columns in (width, width, low, width - low):
-                shapes.append(pltpu.VMEM((*rest, 16, columns), jnp.bfloat16))
-            if phase < 2:
-                shapes.append(pltpu.VMEM((*rest, 16, width), jnp.bfloat16))
+            columns = (width, width, low, width - low) if phase == 0 else (width, width, width)
+            for count in columns + (width,) * (phase < 2):
+                shapes.append(pltpu.VMEM((*rest, 16, count), jnp.bfloat16))
     return shapes + [pltpu.SemaphoreType.DMA((54,)), pltpu.SemaphoreType.DMA((54,))]
 
 
@@ -114,12 +113,12 @@
         for _ in range(3):
             self.slots.append([])
             for phase in range(3):
-                count = 5 if phase < 2 else 4
+                count = (5, 4, 3)[phase]
                 self.slots[-1].append(scratch[:count])
                 scratch = scratch[count:]
         self.data = [[part] for part in parts]
         for part in range(3):
-            self.data[part] += [self.slots[part][phase][4] for phase in range(2)]
+            self.data[part] += [self.slots[part][0][4], self.slots[part][1][3]]
         self.finish = finish
         self.copies = {}
 
@@ -145,6 +144,13 @@
 
     def open(self, part, phase):
         _, right, left, opposite, to_right, to_left = self.around(part, phase)
+        if phase:
+            axis, rest, at = ORDERS[part][phase]
+            across = self.place.device(axis, opposite)
+            for message, (j, to) in enumerate(((opposite, across), (right, to_right), (left, to_left))):
+                source = self.data[part][phase].at[(*at(j, (slice(None),) * len(rest)),)]
+                self.copy(part, phase, message, source, self.slots[part][phase][message], to)
+            return
         from_left, from_right, relay_left, relay_right = self.slots[part][phase][:4]
         low, high = pl.ds(0, self.low), pl.ds(self.low, self.width - self.low)
         self.copy(part, phase, 0, self.view(part, phase, opposite, True), relay_left, to_right)
@@ -176,15 +182,16 @@
     def close(self, part, phase):
         i = self.around(part, phase)[0]
         _, rest, at = ORDERS[part][phase]
-        from_left, from_right = self.slots[part][phase][:2]
+        arrived = self.slots[part][phase][: 3 if phase else 2]
         data = self.data[part][phase]
-        for message in (2, 3, 4, 5):
+        for message in (0, 1, 2) if phase else (2, 3, 4, 5):
             self.copies[part, phase, message].wait_recv()
 
         def add(r):
             there = (*r, slice(None), slice(None))
             total = data[(*at(i, r), slice(None), slice(None))].astype(jnp.float32)
-            total = total + from_left[there].astype(jnp.float32) + from_right[there].astype(jnp.float32)
+            for slot in arrived:
+                total = total + slot[there].astype(jnp.float32)
             if phase < 2:
                 self.data[part][phase + 1][there] = total.astype(jnp.bfloat16)
             else:
@@ -192,16 +199,15 @@
 
         over(rest, add)
 
-    def steps(self):
-        for phase in range(3):
-            for part in range(3):
-                self.relay(part, phase)
-                yield
-            for part in range(3):
-                self.close(part, phase)
-                if phase < 2:
-                    self.open(part, phase + 1)
-                yield
+    def relays(self):
+        for part in range(3):
+            self.relay(part, 0)
+
+    def advance(self, phase):
+        for part in range(3):
+            self.close(part, phase)
+            if phase < 2:
+                self.open(part, phase + 1)
 
     def drain(self):
         for made in self.copies.values():
@@ -274,7 +280,10 @@
         load.start()
 
     above, below = (member, lax.rem(space + 1, 16)), (member, lax.rem(space + 15, 16))
-    others = [lax.rem(member + k, 8) for k in range(1, 8)]
+    others = [
+        lax.rem(place.y + 4 - back, 4) * 2 + lax.rem(member + turn, 2)
+        for back, turn in ((0, 1), (1, 0), (1, 1), (2, 0), (2, 1), (3, 0), (3, 1))
+    ]
     entry_barrier([above, below, place.partner, *place.neighbours(), *[(other, space) for other in others]])
     sent_copies = []
 
@@ -310,11 +319,34 @@
     for columns in in_columns():
         r.queries[:, columns] = dot_nn(r.normed[...], r.w_qkv[:, columns]).astype(jnp.bfloat16)
 
+    def push_edges(source, target, sems):
+        made = []
+        for m in range(2):
+            made.append(push(source.at[pl.ds(m * 128 + 64, 64)], target.at[m, pl.ds(0, 64)], sems, (0, m), above))
+            made.append(push(source.at[pl.ds(m * 128, 64)], target.at[m, pl.ds(64, 64)], sems, (1, m), below))
+        return made
+
+    queries_here = push_edges(r.queries, r.queries_h, r.query_sems)
+    for part in range(2):
+        loads[1 + part].wait()
+        for n in range(4):
+            at = slice(part * 1024 + n * 256, part * 1024 + n * 256 + 256)
+            value = dot_nn(r.normed[...], r.w_qkv[:, slice(at.start + 1024, at.stop + 1024)]).astype(jnp.bfloat16)
+            r.kv[0, 0:128, at] = value[:128]
+            r.kv[1, 0:128, at] = value[128:]
+
     row = lax.broadcasted_iota(jnp.int32, (256, 256), 0) % 128
     key = lax.broadcasted_iota(jnp.int32, (256, 256), 1)
-    token = space * 128 - 64 + key
-    inside = (key >= row) & (key <= row + 128) & (token >= 0) & (token < 2048)
+    offset = jnp.where(key < 128, key, jnp.where(key < 192, key - 192, key - 64))
+    token = space * 128 + offset
+    inside = (offset >= row - 64) & (offset <= row + 64) & (token >= 0) & (token < 2048)
     r.window[...] = jnp.where(inside, 1.0, 0.0)
+    row = lax.broadcasted_iota(jnp.int32, (256, 128), 0) % 128
+    key = lax.broadcasted_iota(jnp.int32, (256, 128), 1)
+    offset = jnp.where(row < 64, row - 64, row + 64)
+    token = space * 128 + offset
+    inside = (key >= offset - 64) & (key <= offset + 64) & (token >= 0) & (token < 2048)
+    r.window_h[...] = jnp.where(inside, 1.0, 0.0)
     for group, columns in enumerate(in_columns()):
         local = r.edge_token[:, columns] - space * 128
         weight = r.edge_weight[:, columns]
@@ -327,27 +359,23 @@
         r.edges_t[group] = both
         r.edges[group] = both.T
 
-    for made in halo_tokens:
-        made.wait_recv()
-    for m in range(2):
-        r.halo[m] = normalised(r.halo[m])[0].astype(jnp.bfloat16)
-    every = jnp.concatenate([r.normed[...], r.halo[0], r.halo[1]], axis=0)
-    for part in range(2):
-        loads[1 + part].wait()
-        for n in range(4):
-            at = slice(part * 1024 + n * 256, part * 1024 + n * 256 + 256)
-            value = dot_nn(every, r.w_qkv[:, slice(at.start + 1024, at.stop + 1024)]).astype(jnp.bfloat16)
-            for m in range(2):
-                edge = 256 + m * 128
-                r.kv[m, 0:64, at] = value[edge : edge + 64]
-                r.kv[m, 64:192, at] = value[m * 128 : m * 128 + 128]
-                r.kv[m, 192:256, at] = value[edge + 64 : edge + 128]
+    def edge_keys(m):
+        for made in halo_tokens[2 * m : 2 * m + 2]:
+            made.wait_recv()
+        edges_normed = normalised(r.halo[m])[0].astype(jnp.bfloat16)
+        for n in range(8):
+            at = slice(n * 256, n * 256 + 256)
+            value = dot_nn(edges_normed, r.w_qkv[:, slice(at.start + 1024, at.stop + 1024)])
+            r.kv[m, 128:256, at] = value.astype(jnp.bfloat16)
 
     first = lax.broadcasted_iota(jnp.int32, (128, 128), 1) < 64
 
     def stacked(value):
         zero = jnp.zeros_like(value)
         return jnp.concatenate([jnp.where(first, value, zero), jnp.where(first, zero, value)], axis=0)
+
+    lane = lax.broadcasted_iota(jnp.int32, (256, 128), 1)
+    r.scales[...] = jnp.zeros_like(r.scales)
 
     def attend(i, carry):
         m, n = i // 8, lax.rem(i, 8)
@@ -356,14 +384,27 @@
         token_rows = pl.ds(pl.multiple_of(m * 128, 128), 128)
         scores = dot_nt(stacked(r.queries[token_rows, columns]), r.kv[m, :, columns])
         expo = jnp.where(r.window[...] > 0.0, jnp.exp(scores * 0.125), 0.0)
-        probs = expo / jnp.sum(expo, axis=-1, keepdims=True)
+        scale = 1.0 / jnp.sum(expo, axis=-1, keepdims=True)
+        probs = expo * scale
         r.probs[i] = probs
+        r.scales[...] = jnp.where(lane == i, scale, r.scales[...])
         result = dot_nn(probs.astype(jnp.bfloat16), r.kv[m, :, values])
         r.att[token_rows, columns] = jnp.where(first, result[:128], result[128:]).astype(jnp.bfloat16)
         return carry
 
-    lax.fori_loop(0, 16, attend, 0, unroll=2)
+    for m in range(2):
+        edge_keys(m)
+        lax.fori_loop(m * 8, m * 8 + 8, attend, 0, unroll=2)
     att_here = pair(r.att, r.att_2)
+    edge_here = queries_here + push_edges(r.att, r.att_h, r.att_sems)
+    for head in range(2):
+        begin = head * 128
+        edge_here.append(push(
+            r.scales.at[pl.ds(begin + 64, 64)], r.scales_h.at[pl.ds(begin, 64)], r.scale_sems, (0, head), above
+        ))
+        edge_here.append(push(
+            r.scales.at[pl.ds(begin, 64)], r.scales_h.at[pl.ds(begin + 64, 64)], r.scale_sems, (1, head), below
+        ))
     loads[3].wait()
     for columns in in_columns():
         value = r.tokens[:, columns].astype(jnp.float32) + dot_nn(r.att[...], r.w_out[:, columns])
@@ -414,6 +455,15 @@
             r.held[member] = r.sent[member]
     r.area_here[...] = jnp.broadcast_to(r.area[pl.ds(member, 1), :], (128, 128)).T
     loads[5].wait()
+
+    def turn(source, target, begin):
+        for columns in in_columns():
+            target[columns, begin : begin + 256] = source[:, columns].T
+
+    turn(r.states, r.states_t, 0)
+    states_here.wait_recv()
+    turn(r.states_2, r.states_t, 256)
+    turn(r.att, r.att_t, 0)
     for other in others:
         take(r.held, 0, other).wait_recv()
 
@@ -449,6 +499,11 @@
         give(r.sent_back, r.held_back, 1, other).start()
     r.held_back[member] = r.sent_back[member]
 
+    att_here.wait_recv()
+    turn(r.att_2, r.att_t, 256)
+    turn(r.normed, r.normed_t, 0)
+    normed_here.wait_recv()
+    turn(r.normed_2, r.normed_t, 256)
     r.gathered[...] = jnp.zeros_like(r.gathered)
     r.turned[...] = jnp.zeros_like(r.turned)
     for n in range(4):
@@ -459,18 +514,19 @@
             take(r.held_back, 1, 2 * group).wait_recv()
             take(r.held_back, 1, 2 * group + 1).wait_recv()
 
-        def backward(b, carry, group=group):
+        def backward(b, group=group):
             grad = jnp.concatenate([r.held_back[2 * group, b], r.held_back[2 * group + 1, b]], axis=0)
-            token_rows = pl.ds(pl.multiple_of(b * 128, 128), 128)
+            grad_t = grad.T
+            token_rows = pl.ds(b * 128, 128)
             for columns in in_columns():
                 hidden = dot_nt(grad, r.readout[columns, :])
                 grad_pre = (hidden * r.slope[b, group, :, columns].astype(jnp.float32)).astype(jnp.bfloat16)
                 both = dot_nn(r.edges_t[group], grad_pre)
                 r.gathered[token_rows, columns] += both[:128] + both[128:]
-                r.turned[:, columns] += dot_tn(grad, r.active[b, group, :, columns])
-            return carry
-
-        lax.fori_loop(0, 2, backward, 0)
+                r.turned[:, columns] += dot_nn(grad_t, r.active[b, group, :, columns])
+
+        for b in range(2):
+            backward(b)
 
     mine = pl.ds(pl.multiple_of(core * 512, 512), 512)
     other_half = pl.ds(pl.multiple_of((1 - core) * 512, 512), 512)
@@ -487,115 +543,143 @@
         r.grad_sb[:, rows] = value.astype(jnp.bfloat16)
     grad_s_here = pair(r.grad_sb.at[:, other_half], r.grad_s2)
 
+    for rows in in_columns():
+        r.grad_att[:, rows] = dot_nt(r.grad_sb[...], r.w_out[rows, :]).astype(jnp.bfloat16)
+    edge_here += push_edges(r.grad_att, r.grad_att_h, r.grad_att_sems)
+
     def early_tile(tile, y, value):
         columns = slice(tile % 3 * 128, tile % 3 * 128 + 128)
         r.early_data[tile // 3, y, :, :, :, :, columns] = value.astype(jnp.bfloat16).reshape(2, 2, 4, 16, 128)
 
-    states_here.wait_recv()
     gather_here.wait_recv()
+    both = jnp.concatenate([r.gather_b[:, mine], r.gather_2[...]], axis=0)
     for y, rows in enumerate(in_columns()):
-        value = dot_tn(r.states[:, rows], r.gather_b[:, mine]) + dot_tn(r.states_2[:, rows], r.gather_2[...])
+        value = dot_nn(r.states_t[rows, :], both)
         for tile in range(4):
             early_tile(tile, y, value[:, tile * 128 : tile * 128 + 128])
     readout_here.wait_recv()
     for y, rows in enumerate(in_columns()):
         early_tile(8, y, r.readout_grad[rows, :].astype(jnp.float32) + r.readout_2[rows, :].astype(jnp.float32))
-    att_here.wait_recv()
     grad_s_here.wait_recv()
+    both = jnp.concatenate([r.grad_sb[:, mine], r.grad_s2[...]], axis=0)
     for y, rows in enumerate(in_columns()):
-        value = dot_tn(r.att[:, rows], r.grad_sb[:, mine]) + dot_tn(r.att_2[:, rows], r.grad_s2[...])
+        value = dot_nn(r.att_t[rows, :], both)
         for tile in range(4):
             early_tile(4 + tile, y, value[:, tile * 128 : tile * 128 + 128])
 
-    def early_finish(part, total):
-        r.early_final[:, :, part * 384 : part * 384 + 384] = total.reshape(2, 8, 384)
-
-    def late_finish(part, total):
-        r.late_final[:, :, part * 512 : part * 512 + 512] = total.reshape(2, 8, 512)
-
-    split = len(ring_scratch) // 2
-    early = RingSum(place, 384, [r.early_data.at[part] for part in range(3)], ring_scratch[:split], early_finish)
-    late = RingSum(place, 512, [r.late_data.at[part] for part in range(3)], ring_scratch[split:], late_finish)
+    def ring_sum(data, final, width, scratch):
+        def finish(part, total):
+            final[:, :, part * width : part * width + width] = total.reshape(2, 8, width)
+
+        return RingSum(place, width, [data.at[part] for part in range(3)], scratch, finish)
+
+    third = len(ring_scratch) // 3
+    early = ring_sum(r.early_data, r.early_final, 384, ring_scratch[:third])
+    late = [
+        ring_sum(r.late_data.at[g], r.late_final.at[g], 256, ring_scratch[third * (1 + g) : third * (2 + g)])
+        for g in range(2)
+    ]
     for part in range(3):
         early.open(part, 0)
-    early_steps = early.steps()
-
-    for rows in in_columns():
-        r.grad_att[:, rows] = dot_nt(r.grad_sb[...], r.w_out[rows, :]).astype(jnp.bfloat16)
-
-    def attend_back(m, n, carry):
+
+    def attend_back(i, carry):
+        n, m = i // 2, lax.rem(i, 2)
         start = pl.multiple_of(n * 128, 128)
         columns, values = pl.ds(start, 128), pl.ds(start + 1024, 128)
-        token_rows = pl.ds(m * 128, 128)
+        token_rows = pl.ds(pl.multiple_of(m * 128, 128), 128)
+        turn_index = m * 8 + n
         queries = stacked(r.queries[token_rows, columns])
         grads = stacked(r.grad_att[token_rows, columns])
-        probs = r.probs[m * 8 + n]
+        att = r.att[token_rows, columns].astype(jnp.float32)
+        inner = jnp.sum(grads.astype(jnp.float32) * jnp.concatenate([att, att], axis=0), axis=-1, keepdims=True)
+        probs = r.probs[turn_index]
         dprob = dot_nt(grads, r.kv[m, :, values])
-        inner = jnp.sum(probs * dprob, axis=-1, keepdims=True)
         dscore = (probs * (dprob - inner) * 0.125).astype(jnp.bfloat16)
         grad_q = dot_nn(dscore, r.kv[m, :, columns])
         r.grad_qkv[token_rows, columns] = jnp.where(first, grad_q[:128], grad_q[128:]).astype(jnp.bfloat16)
-        for value, at in (
-            (dot_tn(dscore, queries), columns), (dot_tn(probs.astype(jnp.bfloat16), grads), values)
-        ):
-            r.lower[m, :, at] = value[:64].astype(jnp.bfloat16)
-            r.middle[token_rows, at] = value[64:192]
-            r.upper[m, :, at] = value[192:].astype(jnp.bfloat16)
+
+        queries_h = stacked(r.queries_h[m, :, columns])
+        grads_h = stacked(r.grad_att_h[m, :, columns])
+        att = r.att_h[m, :, columns].astype(jnp.float32)
+        inner = jnp.sum(grads_h.astype(jnp.float32) * jnp.concatenate([att, att], axis=0), axis=-1, keepdims=True)
+        scale = jnp.sum(jnp.where(lane == turn_index, r.scales_h[...], 0.0), axis=-1, keepdims=True)
+        scores = dot_nt(queries_h, r.kv[m, 0:128, columns])
+        probs_h = jnp.where(r.window_h[...] > 0.0, jnp.exp(scores * 0.125) * scale, 0.0)
+        dprob = dot_nt(grads_h, r.kv[m, 0:128, values])
+        dscore_h = (probs_h * (dprob - inner) * 0.125).astype(jnp.bfloat16)
+
+        grad_k = dot_tn(
+            jnp.concatenate([dscore[:, :128], dscore_h], axis=0), jnp.concatenate([queries, queries_h], axis=0)
+        )
+        grad_v = dot_tn(
+            jnp.concatenate([probs[:, :128].astype(jnp.bfloat16), probs_h.astype(jnp.bfloat16)], axis=0),
+            jnp.concatenate([grads, grads_h], axis=0),
+        )
+        r.grad_qkv[token_rows, values] = grad_k.astype(jnp.bfloat16)
+        r.grad_qkv[token_rows, pl.ds(start + 2048, 128)] = grad_v.astype(jnp.bfloat16)
         return carry
 
-    halos = []
-    for m in range(2):
-        for half in range(2):
-            lax.fori_loop(half * 4, half * 4 + 4, functools.partial(attend_back, m), 0, unroll=2)
-            for _ in range(4):
-                next(early_steps, None)
-        halos.append(push(r.lower.at[m], r.from_above.at[m], r.halo_sems, (0, m), below))
-        halos.append(push(r.upper.at[m], r.from_below.at[m], r.halo_sems, (1, m), above))
-
-    def swap(part):
-        at = pl.ds(pl.multiple_of(part * 1024 + (1 - core) * 512, 512), 512)
-        return pair(r.grad_qkv.at[:, at], r.grad_qkv2.at[part])
-
-    def late_product(part):
-        own = r.grad_qkv[:, pl.ds(pl.multiple_of(part * 1024 + core * 512, 512), 512)]
-        for y, rows in enumerate(in_columns()):
-            value = dot_tn(r.normed[:, rows], own) + dot_tn(r.normed_2[:, rows], r.grad_qkv2[part])
-            r.late_data[part, y] = value.astype(jnp.bfloat16).reshape(2, 2, 4, 16, 512)
-        late.open(part, 0)
-
-    swaps = [swap(0)]
-    normed_here.wait_recv()
-    swaps[0].wait_recv()
-    late_product(0)
-    for made in halos:
+    def own_columns(group, part, which):
+        return pl.ds(pl.multiple_of(part * 1024 + group * 512 + which * 256, 256), 256)
+
+    def swap(group):
+        return [
+            pair(r.grad_qkv.at[:, own_columns(group, part, 1 - core)], r.grad_qkv2.at[group, part])
+            for part in range(3)
+        ]
+
+    def late_products(group, swaps):
+        for part in range(3):
+            swaps[part].wait_recv()
+            both = jnp.concatenate(
+                [r.grad_qkv[:, own_columns(group, part, core)], r.grad_qkv2[group, part]], axis=0
+            )
+            for y, rows in enumerate(in_columns()):
+                value = dot_nn(r.normed_t[rows, :], both)
+                r.late_data[group, part, y] = value.astype(jnp.bfloat16).reshape(2, 2, 4, 16, 256)
+            late[group].open(part, 0)
+
+    for made in edge_here:
         made.wait_recv()
-    for m in range(2):
-        low_rows, high_rows = slice(m * 128, m * 128 + 64), slice(m * 128 + 64, m * 128 + 128)
-        for part in range(2):
-            at, into = slice(part * 1024, part * 1024 + 1024), slice(part * 1024 + 1024, part * 1024 + 2048)
-            for rows, arrived in ((low_rows, r.from_below), (high_rows, r.from_above)):
-                total = r.middle[rows, at] + arrived[m, :, at].astype(jnp.float32)
-                r.grad_qkv[rows, into] = total.astype(jnp.bfloat16)
-    swaps += [swap(1), swap(2)]
-    for _ in early_steps:
-        pass
-    final_sums = [push(r.early_final.at[1 - core], r.early_other, r.final_sems, (0,), place.partner)]
-    for part in (1, 2):
-        swaps[part].wait_recv()
-        late_product(part)
-    late_steps = late.steps()
-    for rows in in_columns():
-        r.middle[:, rows] = dot_nt(r.grad_qkv[...], r.w_qkv[rows, :])
-        next(late_steps, None)
-        next(late_steps, None)
+    lax.fori_loop(0, 8, attend_back, 0)
+    swaps = swap(0)
+    early.relays()
+    lax.fori_loop(8, 12, attend_back, 0)
+    late_products(0, swaps)
+    lax.fori_loop(12, 16, attend_back, 0)
+    swaps = swap(1)
+    early.advance(0)
+    late[0].relays()
+    late_products(1, swaps)
+
+    def back_normed(part):
+        rows = slice(part * 256, part * 256 + 256)
+        r.grad_normed[:, rows] = dot_nt(r.grad_qkv[...], r.w_qkv[rows, :])
+
+    def finals(i):
+        source = (r.early_final, r.late_final.at[0], r.late_final.at[1])[i]
+        target = (r.early_other, r.late_other.at[0], r.late_other.at[1])[i]
+        return push(source.at[1 - core], target, r.final_sems, (i,), place.partner)
+
+    back_normed(0)
+    early.advance(1)
+    back_normed(1)
+    late[0].advance(0)
+    back_normed(2)
+    late[1].relays()
+    back_normed(3)
+    early.advance(2)
+    final_sums = [finals(0)]
     for block in range(4):
         rows = slice(block * 64, block * 64 + 64)
         normal_hat, inverse = normalised(r.tokens[rows, :])
-        back = norm_back(r.middle[rows, :1024], normal_hat, inverse)
+        back = norm_back(r.grad_normed[rows, :], normal_hat, inverse)
         r.grad_tokens[rows, :] = (r.grad_s[rows, :] + back).astype(jnp.bfloat16)
-    for _ in late_steps:
-        pass
-    final_sums.append(push(r.late_final.at[1 - core], r.late_other, r.final_sems, (1,), place.partner))
+    late[0].advance(1)
+    late[1].advance(0)
+    late[0].advance(2)
+    final_sums.append(finals(1))
+    late[1].advance(1)
 
     yours = pl.ds(pl.multiple_of((1 - core) * 512, 512), 512)
     r.grad_hidden_w[:, mine] = r.early_final[core, :, :512]
@@ -604,18 +688,32 @@
     final_sums[0].wait_recv()
     r.grad_hidden_w[:, yours] = r.early_other[:, :512]
     r.grad_out_w[:, yours] = r.early_other[:, 512:1024]
+
+    def place_late(group):
+        for part in range(3):
+            at = slice(part * 256, part * 256 + 256)
+            r.grad_qkv_w[:, own_columns(group, part, core)] = r.late_final[group, core, :, at]
+            r.grad_qkv_w[:, own_columns(group, part, 1 - core)] = r.late_other[group, :, at]
+
+    late[1].advance(2)
+    final_sums.append(finals(2))
     final_sums[1].wait_recv()
-    for part in range(3):
-        at = slice(part * 512, part * 512 + 512)
-        for half, rows in ((core, r.late_final[core, :, at]), (1 - core, r.late_other[:, at])):
-            r.grad_qkv_w[:, pl.ds(pl.multiple_of(part * 1024 + half * 512, 512), 512)] = rows
+    place_late(0)
+    final_sums[2].wait_recv()
+    place_late(1)
     for made in sent_copies:
         made.wait_send()
     for other in others:
         give(r.sent, r.held, 0, other).wait_send()
         give(r.sent_back, r.held_back, 1, other).wait_send()
-    early.drain()
-    late.drain()
+    for sums in (early, *late):
+        sums.drain()
+
+
+def handed_on(*refs):
+    count = len(refs) // 2
+    for source, target in zip(refs[:count], refs[count:]):
+        target[...] = source[...]
 
 
 def on_device(
@@ -651,7 +749,10 @@
     scratch = {
         "w_qkv": b16(1024, 3072), "w_out": b16(1024, 1024), "w_hidden": b16(1024, 1024), "truth": f32(128, 128),
         "area_here": f32(128, 128), "halo": b16(2, 128, 1024), "normed": b16(256, 1024), "normed_2": b16(256, 1024),
-        "queries": b16(256, 1024), "kv": b16(2, 256, 2048), "window": f32(256, 256), "probs": f32(16, 256, 256),
+        "queries": b16(256, 1024), "kv": b16(2, 256, 2048), "window": f32(256, 256), "window_h": f32(256, 128), "scales": f32(256, 128), "scales_h": f32(256, 128),
+        "queries_h": b16(2, 128, 1024), "att_h": b16(2, 128, 1024), "grad_att_h": b16(2, 128, 1024),
+        "states_t": b16(1024, 512), "att_t": b16(1024, 512), "normed_t": b16(1024, 512),
+        "probs": f32(16, 256, 256),
         "att": b16(256, 1024), "att_2": b16(256, 1024), "states": b16(256, 1024), "states_2": b16(256, 1024),
         "hidden": b16(2, 256, 1024), "edges": b16(4, 256, 256), "edges_t": b16(4, 256, 256),
         "active": b16(2, 4, 256, 1024), "slope": b16(2, 4, 256, 1024),
@@ -660,13 +761,13 @@
         "gathered": f32(256, 1024), "gather_b": b16(256, 1024), "gather_2": b16(256, 512),
         "grad_s": f32(256, 1024), "grad_sb": b16(256, 1024), "grad_s2": b16(256, 512), "grad_att": b16(256, 1024),
         "readout_grad": b16(1024, 128), "readout_2": b16(1024, 128), "grad_qkv": b16(256, 3072),
-        "grad_qkv2": b16(3, 256, 512), "middle": f32(256, 2048), "lower": b16(2, 64, 2048), "upper": b16(2, 64, 2048),
-        "from_above": b16(2, 64, 2048), "from_below": b16(2, 64, 2048),
-        "early_data": b16(3, *FULL, 16, 384), "late_data": b16(3, *FULL, 16, 512),
-        "early_final": f32(2, 8, 1152), "late_final": f32(2, 8, 1536),
-        "early_other": f32(8, 1152), "late_other": f32(8, 1536),
-        "load_sems": dma((6,)), "token_sems": dma((2, 2, 2)), "pair_sems": dma((2, 9)), "halo_sems": dma((2, 2, 2)),
-        "member_sems": dma((2, 2, 8)), "final_sems": dma((2, 2)),
+        "grad_qkv2": b16(2, 3, 256, 256), "grad_normed": f32(256, 1024),
+        "early_data": b16(3, *FULL, 16, 384), "late_data": b16(2, 3, *FULL, 16, 256),
+        "early_final": f32(2, 8, 1152), "late_final": f32(2, 2, 8, 768),
+        "early_other": f32(8, 1152), "late_other": f32(2, 8, 768),
+        "load_sems": dma((6,)), "token_sems": dma((2, 2, 2)), "pair_sems": dma((2, 12)), "query_sems": dma((2, 2, 2)),
+        "att_sems": dma((2, 2, 2)), "scale_sems": dma((2, 2, 2)), "grad_att_sems": dma((2, 2, 2)),
+        "member_sems": dma((2, 2, 8)), "final_sems": dma((2, 3)),
     }
     names = [*inputs, *outputs, *scratch]
     results = pl.pallas_call(
@@ -674,11 +775,17 @@
         out_shape=tuple(outputs.values()),
         in_specs=[spec for _, spec in inputs.values()],
         out_specs=[vmem] * len(outputs),
-        scratch_shapes=[*scratch.values(), *sum_scratch(384), *sum_scratch(512)],
+        scratch_shapes=[*scratch.values(), *sum_scratch(384), *sum_scratch(256), *sum_scratch(256)],
         compiler_params=pltpu.CompilerParams(
             collective_id=0, has_side_effects=True, vmem_limit_bytes=62 * 2**20
         ),
     )(*[value for value, _ in inputs.values()])
+    results = pl.pallas_call(
+        handed_on,
+        out_shape=tuple(outputs.values()),
+        in_specs=[vmem] * len(outputs),
+        out_specs=[vmem] * len(outputs),
+    )(*results)
     return (results[0].reshape(tokens.shape), *results[1:])
 
 

time: 135 us -> 105 us (0.78)
  Pallas kernels: 127 us -> 104 us
  local copies, waits for them, and re-layouts: 7.43 us -> 0 us
    pallas_call x1, Pallas kernels: 127 us -> 102 us  [on_device(): pl.pallas_call(functools.partial(kernel, names), out_shape=tuple(outputs....]
    unnamed x5 -> x0, local copies, waits for them, and re-layouts: 7.43 us -> none
    pallas_call x0 -> x1, Pallas kernels: none -> 1.97 us  [on_device(): pl.pallas_call(handed_on, out_shape=tuple(outputs.values()), in_specs=[vm...]
where the time goes in v1:
time: 105 us; the launch traced here: 104 us
  Pallas kernels  104 us (99%)
    pallas_call x1, Pallas kernels, on_device(): pl.pallas_call(functools.partial(kernel, names), out_shape=tuple(outputs....  102 us

profile of v1, /device:TPU:1, one launch (start us, length us, event | category | flops | bytes accessed | tf_op | source)
XLA Modules:
  0.0 104.5 jit_solution(6220827454775271506)
XLA Ops:
  0.6 101.8 %shard_map.128 = (bf16[256,1024]{1,0:T(8,128)(2,1)}, f32[8,3072]{1,0:T(8,128)}, f32[8,1024]{1,0:T(8,128)}, f32[8,1024]{1,0:T(8,128)}, f32[8,128]{1,0:T(8,128)}) custom-call(bf16[256,1024]{1,0:T(8,128)(2,1)} %bitcast.5, bf16[1024,3072]{1,0:T(8,128)(2,1)} %refs_1_.1, bf16[1024,1024]{1,0:T(8,128)(2,1)} %refs_2_.1, bf16[1024,1024]{1,0:T(8,128)(2,1)} %refs_3_.1, ...), custom_call_target="tpu_custom_call" | custom-call | tf_op jit(solution)/shard_map/pallas_call | solution.py:773
  102.5 2.0 %shard_map.129 = (bf16[256,1024]{1,0:T(8,128)(2,1)}, f32[8,3072]{1,0:T(8,128)}, f32[8,1024]{1,0:T(8,128)}, f32[8,1024]{1,0:T(8,128)}, f32[8,128]{1,0:T(8,128)}) custom-call(bf16[256,1024]{1,0:T(8,128)(2,1)} %get-tuple-element.15.refs_0_, f32[8,3072]{1,0:T(8,128)} %get-tuple-element.16.refs_1_, f32[8,1024]{1,0:T(8,128)} %get-tuple-element.17.refs_2_, ...), custom_call_target="tpu_custom_call" | custom-call | tf_op jit(solution)/shard_map/pallas_call | solution.py:783

commit v2 on v1

--- a/solution.py
+++ b/solution.py
@@ -30,12 +30,13 @@
     def ring(self, axis):
         return {"x": self.x, "y": self.y, "z": self.z}[axis]
 
-    def device(self, axis, j):
+    def device(self, axis, j, core=None):
+        core = self.core if core is None else core
         if axis == "x":
-            return (self.member, (self.space // 8) * 8 + j * 2 + self.core)
+            return (self.member, (self.space // 8) * 8 + j * 2 + core)
         if axis == "y":
-            return (j * 2 + self.member % 2, self.space)
-        return ((self.member // 2) * 2 + j % 2, (j // 2) * 8 + self.space % 8)
+            return (j * 2 + self.member % 2, (self.space // 2) * 2 + core)
+        return ((self.member // 2) * 2 + j % 2, (j // 2) * 8 + ((self.space % 8) // 2) * 2 + core)
 
     def neighbours(self):
         found = []
@@ -80,11 +81,13 @@
     low = first_columns(width)
     shapes = []
     for order in ORDERS:
-        for phase, (_, rest, _) in enumerate(order):
-            columns = (width, width, low, width - low) if phase == 0 else (width, width, width)
-            for count in columns + (width,) * (phase < 2):
-                shapes.append(pltpu.VMEM((*rest, 16, count), jnp.bfloat16))
-    return shapes + [pltpu.SemaphoreType.DMA((54,)), pltpu.SemaphoreType.DMA((54,))]
+        (_, rest, _), (_, rest_1, _), _ = order
+        for columns in (width, width, low, width - low, width):
+            shapes.append(pltpu.VMEM((*rest, 16, columns), jnp.bfloat16))
+        shapes += [pltpu.VMEM((*rest_1, 16, width), jnp.bfloat16)] * 3
+        shapes.append(pltpu.VMEM((*rest_1, 2, 8, width), jnp.float32))
+        shapes.append(pltpu.VMEM((4, 2, 8, width), jnp.float32))
+    return shapes + [pltpu.SemaphoreType.DMA((60,)), pltpu.SemaphoreType.DMA((60,))]
 
 
 def over(dims, body):
@@ -113,7 +116,7 @@
         for _ in range(3):
             self.slots.append([])
             for phase in range(3):
-                count = (5, 4, 3)[phase]
+                count = (5, 4, 1)[phase]
                 self.slots[-1].append(scratch[:count])
                 scratch = scratch[count:]
         self.data = [[part] for part in parts]
@@ -123,7 +126,7 @@
         self.copies = {}
 
     def copy(self, part, phase, message, source, target, device):
-        sem = (part * 3 + phase) * 6 + message
+        sem = part * 20 + (0, 6, 12)[phase] + message
         made = pltpu.make_async_remote_copy(
             src_ref=source, dst_ref=target, send_sem=self.send.at[sem], recv_sem=self.recv.at[sem],
             device_id=device, device_id_type=MESH,
@@ -144,6 +147,20 @@
 
     def open(self, part, phase):
         _, right, left, opposite, to_right, to_left = self.around(part, phase)
+        if phase == 2:
+            axis, _, at = ORDERS[part][2]
+            i, core = self.place.ring(axis), self.place.core
+            data, slots = self.data[part][2], self.slots[part][2][0]
+            for step in (2, 1, 3, 0):
+                j = (i + step) % 4
+                for message, to in ((2 * step, core), (2 * step + 1, 1 - core)):
+                    if message:
+                        self.copy(
+                            part, 2, message, data.at[(*at(j, ()), to)], slots.at[i, core],
+                            self.place.device(axis, j, to),
+                        )
+            slots[i, core] = data[(*at(i, ()), core)]
+            return
         if phase:
             axis, rest, at = ORDERS[part][phase]
             across = self.place.device(axis, opposite)
@@ -182,6 +199,12 @@
     def close(self, part, phase):
         i = self.around(part, phase)[0]
         _, rest, at = ORDERS[part][phase]
+        if phase == 2:
+            for message in range(1, 8):
+                self.copies[part, 2, message].wait_recv()
+            slots = self.slots[part][2][0]
+            self.finish(part, (slots[0] + slots[1]) + (slots[2] + slots[3]))
+            return
         arrived = self.slots[part][phase][: 3 if phase else 2]
         data = self.data[part][phase]
         for message in (0, 1, 2) if phase else (2, 3, 4, 5):
@@ -192,10 +215,11 @@
             total = data[(*at(i, r), slice(None), slice(None))].astype(jnp.float32)
             for slot in arrived:
                 total = total + slot[there].astype(jnp.float32)
-            if phase < 2:
-                self.data[part][phase + 1][there] = total.astype(jnp.bfloat16)
+            if phase == 0:
+                self.data[part][1][there] = total.astype(jnp.bfloat16)
             else:
-                self.finish(part, total)
+                halves = total.reshape(*total.shape[:-2], 2, 8, self.width)
+                self.data[part][2][(*r, slice(None), slice(None), slice(None))] = halves
 
         over(rest, add)
 
@@ -280,10 +304,9 @@
         load.start()
 
     above, below = (member, lax.rem(space + 1, 16)), (member, lax.rem(space + 15, 16))
-    others = [
-        lax.rem(place.y + 4 - back, 4) * 2 + lax.rem(member + turn, 2)
-        for back, turn in ((0, 1), (1, 0), (1, 1), (2, 0), (2, 1), (3, 0), (3, 1))
-    ]
+    home = member // 4
+    nearby = [home * 4 + lax.rem(member + k, 4) for k in range(1, 4)]
+    others = nearby + [(1 - home) * 4 + lax.rem(member + k, 4) for k in range(4)]
     entry_barrier([above, below, place.partner, *place.neighbours(), *[(other, space) for other in others]])
     sent_copies = []
 
@@ -356,8 +379,15 @@
             matrix = matrix + jnp.where(local[slot : slot + 1] == places, weight[slot : slot + 1], 0.0)
         high = matrix.astype(jnp.bfloat16)
         both = jnp.concatenate([high, (matrix - high.astype(jnp.float32)).astype(jnp.bfloat16)], axis=0)
-        r.edges_t[group] = both
-        r.edges[group] = both.T
+        turned = both.T
+        for i in range(2):
+            owner = 2 * group + i
+            for half in range(2):
+                begin = i * 128 + half * 64
+                r.edges[half, owner // 4, owner % 4 * 64 : owner % 4 * 64 + 64, :] = turned[begin : begin + 64]
+    for half in range(2):
+        for quad in range(2):
+            r.edges_t[half, quad] = r.edges[half, quad].T
 
     def edge_keys(m):
         for made in halo_tokens[2 * m : 2 * m + 2]:
@@ -417,42 +447,43 @@
             r.hidden[m, 0:128, columns] = value[m * 128 : m * 128 + 128]
             r.hidden[m, 128:256, columns] = value[m * 128 : m * 128 + 128]
 
-    home = member // 2
-
-    def give(source, target, i, to):
+    def give(source, target, i, half, to):
+        rows = pl.ds(half * 64, 64)
         return pltpu.make_async_remote_copy(
-            src_ref=source.at[to], dst_ref=target.at[member], send_sem=r.member_sems.at[i, 0, to],
-            recv_sem=r.member_sems.at[i, 1, member], device_id=(to, space), device_id_type=MESH,
+            src_ref=source.at[to, :, rows], dst_ref=target.at[member, :, rows],
+            send_sem=r.member_sems.at[i, half, 0, to], recv_sem=r.member_sems.at[i, half, 1, member],
+            device_id=(to, space), device_id_type=MESH,
         )
 
-    def take(target, i, source):
+    def take(target, i, half, source):
+        rows = pl.ds(half * 64, 64)
         return pltpu.make_async_remote_copy(
-            src_ref=target.at[source], dst_ref=target.at[source], send_sem=r.member_sems.at[i, 0, source],
-            recv_sem=r.member_sems.at[i, 1, source], device_id=(source, space), device_id_type=MESH,
+            src_ref=target.at[source, :, rows], dst_ref=target.at[source, :, rows],
+            send_sem=r.member_sems.at[i, half, 0, source], recv_sem=r.member_sems.at[i, half, 1, source],
+            device_id=(source, space), device_id_type=MESH,
         )
 
-    for n in range(4):
-        group = lax.rem(home + 1 + n, 4)
-
-        def forward(b, carry, group=group):
-            forecast = jnp.zeros((256, 128), jnp.float32)
-            for columns in in_columns():
-                value, derivative = gelu_both(dot_nn(r.edges[group], r.hidden[b, :, columns]))
-                value = value.astype(jnp.bfloat16)
-                r.active[b, group, :, columns] = value
-                r.slope[b, group, :, columns] = derivative.astype(jnp.bfloat16)
-                forecast = forecast + dot_nn(value, r.readout[columns, :])
-            r.sent[2 * group, b] = forecast[:128].astype(jnp.bfloat16)
-            r.sent[2 * group + 1, b] = forecast[128:].astype(jnp.bfloat16)
-            return carry
-
-        lax.fori_loop(0, 2, forward, 0)
-        if n < 3:
-            give(r.sent, r.held, 0, 2 * group).start()
-            give(r.sent, r.held, 0, 2 * group + 1).start()
-        else:
-            give(r.sent, r.held, 0, 2 * group + 1 - lax.rem(member, 2)).start()
-            r.held[member] = r.sent[member]
+    for half in range(2):
+        rows = slice(half * 64, half * 64 + 64)
+        for n in range(2):
+            quad = 1 - home if n == 0 else home
+
+            def forward(b, carry, half=half, quad=quad, rows=rows):
+                forecast = jnp.zeros((256, 128), jnp.float32)
+                for columns in in_columns():
+                    value, derivative = gelu_both(dot_nn(r.edges[half, quad], r.hidden[b, :, columns]))
+                    value = value.astype(jnp.bfloat16)
+                    r.active[b, half, quad, :, columns] = value
+                    r.slope[b, half, quad, :, columns] = derivative.astype(jnp.bfloat16)
+                    forecast = forecast + dot_nn(value, r.readout[columns, :])
+                for i in range(4):
+                    r.sent[4 * quad + i, b, rows] = forecast[i * 64 : i * 64 + 64].astype(jnp.bfloat16)
+                return carry
+
+            lax.fori_loop(0, 2, forward, 0)
+            for to in others[3:] if n == 0 else nearby:
+                give(r.sent, r.held, 0, half, to).start()
+        r.held[member, :, rows] = r.sent[member, :, rows]
     r.area_here[...] = jnp.broadcast_to(r.area[pl.ds(member, 1), :], (128, 128)).T
     loads[5].wait()
 
@@ -464,8 +495,6 @@
     states_here.wait_recv()
     turn(r.states_2, r.states_t, 256)
     turn(r.att, r.att_t, 0)
-    for other in others:
-        take(r.held, 0, other).wait_recv()
 
     multiplier = math.sqrt(16 / 16384)
     eps_fair = (1.0 - ALPHA) / 16
@@ -494,36 +523,38 @@
             r.sent_back[j // 2, j % 2, rows, :] = jnp.concatenate(found[j], axis=0).astype(jnp.bfloat16)
         return carry
 
-    lax.fori_loop(0, 8, score, 0)
-    for other in others:
-        give(r.sent_back, r.held_back, 1, other).start()
-    r.held_back[member] = r.sent_back[member]
-
-    att_here.wait_recv()
-    turn(r.att_2, r.att_t, 256)
-    turn(r.normed, r.normed_t, 0)
+    for half in range(2):
+        rows = slice(half * 64, half * 64 + 64)
+        for other in others:
+            take(r.held, 0, half, other).wait_recv()
+        lax.fori_loop(half * 4, half * 4 + 4, score, 0)
+        for other in others:
+            give(r.sent_back, r.held_back, 1, half, other).start()
+        r.held_back[member, :, rows] = r.sent_back[member, :, rows]
+        if half == 0:
+            att_here.wait_recv()
+            turn(r.att_2, r.att_t, 256)
+            turn(r.normed, r.normed_t, 0)
     normed_here.wait_recv()
     turn(r.normed_2, r.normed_t, 256)
     r.gathered[...] = jnp.zeros_like(r.gathered)
     r.turned[...] = jnp.zeros_like(r.turned)
-    for n in range(4):
-        group = lax.rem(home + n, 4)
-        if n == 0:
-            take(r.held_back, 1, 2 * group + 1 - lax.rem(member, 2)).wait_recv()
-        else:
-            take(r.held_back, 1, 2 * group).wait_recv()
-            take(r.held_back, 1, 2 * group + 1).wait_recv()
-
-        def backward(b, group=group):
-            grad = jnp.concatenate([r.held_back[2 * group, b], r.held_back[2 * group + 1, b]], axis=0)
+    for half, n in ((0, 0), (0, 1), (1, 0), (1, 1)):
+        quad = home if n == 0 else 1 - home
+        for other in nearby if n == 0 else others[3:]:
+            take(r.held_back, 1, half, other).wait_recv()
+
+        def backward(b, half=half, quad=quad):
+            rows = slice(half * 64, half * 64 + 64)
+            grad = jnp.concatenate([r.held_back[4 * quad + i, b, rows] for i in range(4)], axis=0)
             grad_t = grad.T
             token_rows = pl.ds(b * 128, 128)
             for columns in in_columns():
                 hidden = dot_nt(grad, r.readout[columns, :])
-                grad_pre = (hidden * r.slope[b, group, :, columns].astype(jnp.float32)).astype(jnp.bfloat16)
-                both = dot_nn(r.edges_t[group], grad_pre)
+                grad_pre = (hidden * r.slope[b, half, quad, :, columns].astype(jnp.float32)).astype(jnp.bfloat16)
+                both = dot_nn(r.edges_t[half, quad], grad_pre)
                 r.gathered[token_rows, columns] += both[:128] + both[128:]
-                r.turned[:, columns] += dot_nn(grad_t, r.active[b, group, :, columns])
+                r.turned[:, columns] += dot_nn(grad_t, r.active[b, half, quad, :, columns])
 
         for b in range(2):
             backward(b)
@@ -569,7 +600,7 @@
 
     def ring_sum(data, final, width, scratch):
         def finish(part, total):
-            final[:, :, part * width : part * width + width] = total.reshape(2, 8, width)
+            final[:, :, part * width : part * width + width] = total
 
         return RingSum(place, width, [data.at[part] for part in range(3)], scratch, finish)
 
@@ -598,23 +629,28 @@
         grad_q = dot_nn(dscore, r.kv[m, :, columns])
         r.grad_qkv[token_rows, columns] = jnp.where(first, grad_q[:128], grad_q[128:]).astype(jnp.bfloat16)
 
+        local = pl.multiple_of(lax.rem(n, 4) * 128, 128)
+        r.gathered[token_rows, pl.ds(local, 128)] = dot_tn(dscore[:, :128], queries)
+        r.gathered[token_rows, pl.ds(local + 512, 128)] = dot_tn(probs[:, :128].astype(jnp.bfloat16), grads)
+        return carry
+
+    def attend_back_edges(i, carry):
+        n, m = i // 2, lax.rem(i, 2)
+        start = pl.multiple_of(n * 128, 128)
+        columns, values = pl.ds(start, 128), pl.ds(start + 1024, 128)
+        token_rows = pl.ds(pl.multiple_of(m * 128, 128), 128)
         queries_h = stacked(r.queries_h[m, :, columns])
         grads_h = stacked(r.grad_att_h[m, :, columns])
         att = r.att_h[m, :, columns].astype(jnp.float32)
         inner = jnp.sum(grads_h.astype(jnp.float32) * jnp.concatenate([att, att], axis=0), axis=-1, keepdims=True)
-        scale = jnp.sum(jnp.where(lane == turn_index, r.scales_h[...], 0.0), axis=-1, keepdims=True)
+        scale = jnp.sum(jnp.where(lane == m * 8 + n, r.scales_h[...], 0.0), axis=-1, keepdims=True)
         scores = dot_nt(queries_h, r.kv[m, 0:128, columns])
         probs_h = jnp.where(r.window_h[...] > 0.0, jnp.exp(scores * 0.125) * scale, 0.0)
         dprob = dot_nt(grads_h, r.kv[m, 0:128, values])
         dscore_h = (probs_h * (dprob - inner) * 0.125).astype(jnp.bfloat16)
-
-        grad_k = dot_tn(
-            jnp.concatenate([dscore[:, :128], dscore_h], axis=0), jnp.concatenate([queries, queries_h], axis=0)
-        )
-        grad_v = dot_tn(
-            jnp.concatenate([probs[:, :128].astype(jnp.bfloat16), probs_h.astype(jnp.bfloat16)], axis=0),
-            jnp.concatenate([grads, grads_h], axis=0),
-        )
+        local = pl.multiple_of(lax.rem(n, 4) * 128, 128)
+        grad_k = r.gathered[token_rows, pl.ds(local, 128)] + dot_tn(dscore_h, queries_h)
+        grad_v = r.gathered[token_rows, pl.ds(local + 512, 128)] + dot_tn(probs_h.astype(jnp.bfloat16), grads_h)
         r.grad_qkv[token_rows, values] = grad_k.astype(jnp.bfloat16)
         r.grad_qkv[token_rows, pl.ds(start + 2048, 128)] = grad_v.astype(jnp.bfloat16)
         return carry
@@ -639,14 +675,15 @@
                 r.late_data[group, part, y] = value.astype(jnp.bfloat16).reshape(2, 2, 4, 16, 256)
             late[group].open(part, 0)
 
+    lax.fori_loop(0, 8, attend_back, 0, unroll=2)
     for made in edge_here:
         made.wait_recv()
-    lax.fori_loop(0, 8, attend_back, 0)
+    lax.fori_loop(0, 8, attend_back_edges, 0, unroll=2)
     swaps = swap(0)
     early.relays()
-    lax.fori_loop(8, 12, attend_back, 0)
+    lax.fori_loop(8, 16, attend_back, 0, unroll=2)
     late_products(0, swaps)
-    lax.fori_loop(12, 16, attend_back, 0)
+    lax.fori_loop(8, 16, attend_back_edges, 0, unroll=2)
     swaps = swap(1)
     early.advance(0)
     late[0].relays()
@@ -654,12 +691,7 @@
 
     def back_normed(part):
         rows = slice(part * 256, part * 256 + 256)
-        r.grad_normed[:, rows] = dot_nt(r.grad_qkv[...], r.w_qkv[rows, :])
-
-    def finals(i):
-        source = (r.early_final, r.late_final.at[0], r.late_final.at[1])[i]
-        target = (r.early_other, r.late_other.at[0], r.late_other.at[1])[i]
-        return push(source.at[1 - core], target, r.final_sems, (i,), place.partner)
+        r.gathered[:, rows] = dot_nt(r.grad_qkv[...], r.w_qkv[rows, :])
 
     back_normed(0)
     early.advance(1)
@@ -669,43 +701,33 @@
     late[1].relays()
     back_normed(3)
     early.advance(2)
-    final_sums = [finals(0)]
     for block in range(4):
         rows = slice(block * 64, block * 64 + 64)
         normal_hat, inverse = normalised(r.tokens[rows, :])
-        back = norm_back(r.grad_normed[rows, :], normal_hat, inverse)
+        back = norm_back(r.gathered[rows, :], normal_hat, inverse)
         r.grad_tokens[rows, :] = (r.grad_s[rows, :] + back).astype(jnp.bfloat16)
     late[0].advance(1)
     late[1].advance(0)
     late[0].advance(2)
-    final_sums.append(finals(1))
     late[1].advance(1)
 
-    yours = pl.ds(pl.multiple_of((1 - core) * 512, 512), 512)
-    r.grad_hidden_w[:, mine] = r.early_final[core, :, :512]
-    r.grad_out_w[:, mine] = r.early_final[core, :, 512:1024]
-    r.grad_readout[...] = r.early_final[core, :, 1024:]
-    final_sums[0].wait_recv()
-    r.grad_hidden_w[:, yours] = r.early_other[:, :512]
-    r.grad_out_w[:, yours] = r.early_other[:, 512:1024]
-
-    def place_late(group):
+    for half in range(2):
+        at = slice(half * 512, half * 512 + 512)
+        r.grad_hidden_w[:, at] = r.early_final[half, :, :512]
+        r.grad_out_w[:, at] = r.early_final[half, :, 512:1024]
+    r.grad_readout[...] = r.early_final[0, :, 1024:]
+    late[1].advance(2)
+    for group in range(2):
         for part in range(3):
-            at = slice(part * 256, part * 256 + 256)
-            r.grad_qkv_w[:, own_columns(group, part, core)] = r.late_final[group, core, :, at]
-            r.grad_qkv_w[:, own_columns(group, part, 1 - core)] = r.late_other[group, :, at]
-
-    late[1].advance(2)
-    final_sums.append(finals(2))
-    final_sums[1].wait_recv()
-    place_late(0)
-    final_sums[2].wait_recv()
-    place_late(1)
+            for half in range(2):
+                begin = part * 1024 + group * 512 + half * 256
+                r.grad_qkv_w[:, begin : begin + 256] = r.late_final[group, half, :, part * 256 : part * 256 + 256]
     for made in sent_copies:
         made.wait_send()
     for other in others:
-        give(r.sent, r.held, 0, other).wait_send()
-        give(r.sent_back, r.held_back, 1, other).wait_send()
+        for half in range(2):
+            give(r.sent, r.held, 0, half, other).wait_send()
+            give(r.sent_back, r.held_back, 1, half, other).wait_send()
     for sums in (early, *late):
         sums.drain()
 
@@ -754,20 +776,19 @@
         "states_t": b16(1024, 512), "att_t": b16(1024, 512), "normed_t": b16(1024, 512),
         "probs": f32(16, 256, 256),
         "att": b16(256, 1024), "att_2": b16(256, 1024), "states": b16(256, 1024), "states_2": b16(256, 1024),
-        "hidden": b16(2, 256, 1024), "edges": b16(4, 256, 256), "edges_t": b16(4, 256, 256),
-        "active": b16(2, 4, 256, 1024), "slope": b16(2, 4, 256, 1024),
+        "hidden": b16(2, 256, 1024), "edges": b16(2, 2, 256, 256), "edges_t": b16(2, 2, 256, 256),
+        "active": b16(2, 2, 2, 256, 1024), "slope": b16(2, 2, 2, 256, 1024),
         "sent": b16(8, 2, 128, 128), "held": b16(8, 2, 128, 128),
         "sent_back": b16(8, 2, 128, 128), "held_back": b16(8, 2, 128, 128), "turned": f32(128, 1024),
         "gathered": f32(256, 1024), "gather_b": b16(256, 1024), "gather_2": b16(256, 512),
         "grad_s": f32(256, 1024), "grad_sb": b16(256, 1024), "grad_s2": b16(256, 512), "grad_att": b16(256, 1024),
         "readout_grad": b16(1024, 128), "readout_2": b16(1024, 128), "grad_qkv": b16(256, 3072),
-        "grad_qkv2": b16(2, 3, 256, 256), "grad_normed": f32(256, 1024),
+        "grad_qkv2": b16(2, 3, 256, 256),
         "early_data": b16(3, *FULL, 16, 384), "late_data": b16(2, 3, *FULL, 16, 256),
         "early_final": f32(2, 8, 1152), "late_final": f32(2, 2, 8, 768),
-        "early_other": f32(8, 1152), "late_other": f32(2, 8, 768),
         "load_sems": dma((6,)), "token_sems": dma((2, 2, 2)), "pair_sems": dma((2, 12)), "query_sems": dma((2, 2, 2)),
         "att_sems": dma((2, 2, 2)), "scale_sems": dma((2, 2, 2)), "grad_att_sems": dma((2, 2, 2)),
-        "member_sems": dma((2, 2, 8)), "final_sems": dma((2, 3)),
+        "member_sems": dma((2, 2, 2, 8)),
     }
     names = [*inputs, *outputs, *scratch]
     results = pl.pallas_call(

time: 105 us -> 98.4 us (0.937)
  Pallas kernels: 104 us -> 97.6 us
    pallas_call x1, Pallas kernels: 102 us -> 95.6 us  [on_device(): pl.pallas_call(functools.partial(kernel, names), out_shape=tuple(outputs....]
where the time goes in v2:
time: 98.4 us; the launch traced here: 98.2 us
  Pallas kernels  97.6 us (99%)
    pallas_call x1, Pallas kernels, on_device(): pl.pallas_call(functools.partial(kernel, names), out_shape=tuple(outputs....  95.6 us
    pallas_call x1, Pallas kernels, on_device(): pl.pallas_call(handed_on, out_shape=tuple(outputs.values()), in_specs=[vm...  1.97 us

profile of v2, /device:TPU:1, one launch (start us, length us, event | category | flops | bytes accessed | tf_op | source)
XLA Modules:
  0.0 98.2 jit_solution(3596065476617188060)
XLA Ops:
  0.6 95.6 %shard_map.128 = (bf16[256,1024]{1,0:T(8,128)(2,1)}, f32[8,3072]{1,0:T(8,128)}, f32[8,1024]{1,0:T(8,128)}, f32[8,1024]{1,0:T(8,128)}, f32[8,128]{1,0:T(8,128)}) custom-call(bf16[256,1024]{1,0:T(8,128)(2,1)} %bitcast.5, bf16[1024,3072]{1,0:T(8,128)(2,1)} %refs_1_.1, bf16[1024,1024]{1,0:T(8,128)(2,1)} %refs_2_.1, bf16[1024,1024]{1,0:T(8,128)(2,1)} %refs_3_.1, ...), custom_call_target="tpu_custom_call" | custom-call | tf_op jit(solution)/shard_map/pallas_call | solution.py:794
  96.2 2.0 %shard_map.129 = (bf16[256,1024]{1,0:T(8,128)(2,1)}, f32[8,3072]{1,0:T(8,128)}, f32[8,1024]{1,0:T(8,128)}, f32[8,1024]{1,0:T(8,128)}, f32[8,128]{1,0:T(8,128)}) custom-call(bf16[256,1024]{1,0:T(8,128)(2,1)} %get-tuple-element.15.refs_0_, f32[8,3072]{1,0:T(8,128)} %get-tuple-element.16.refs_1_, f32[8,1024]{1,0:T(8,128)} %get-tuple-element.17.refs_2_, ...), custom_call_target="tpu_custom_call" | custom-call | tf_op jit(solution)/shard_map/pallas_call | solution.py:804
